TPU v7x, 32 devices: a whole 2x2x4 slice. The times are simulated.
32 devices in a mesh: wide: 8 (over y, x, core), rep: 4 (over z).
Axes of the slice: x: 2, y: 2, z: 4, core: 2. Of those that a mesh axis runs over, the one named last changes fastest.
Arguments:
- record: bfloat16 [32, 256, 8192], P(('wide', 'rep')), may hold values from -90 to 90
- valid: int32 [32, 8192], P(('wide', 'rep')), may hold values 0 or 1
- sources: int32 [3], replicated, may hold values from 0 to 127
Outputs:
- stacks: float32 [128, 192, 8192], P('rep', None, 'wide')
Inputs may be any that keep to these rules, and one draw needn't show every extreme that they name: `sources`: block b holds the channels 64 * b to 64 * b + 63.
All inputs are finite; a program needn't handle non-finite values. No bound on the sum of `valid` on one device may be relied on, other than what follows from the above.
Results may differ from a plain program's by a relative error of at most 0.0014.
Values may be sent and summed in bfloat16 or wider, within the bound.
A program may use at most 320 MiB of HBM per device.

v0:
```python
import math

import jax
import jax.numpy as jnp
from jax import lax
from jax.sharding import PartitionSpec as P

SRC = 64
NBLK = 3
LAGS = 128
HALF_SMOOTH = 5


EPSILON = 1e-05
LEVEL_SHARE = 0.2


def broadcast(value, axis, source):
    kept = jnp.where(lax.axis_index(axis) == source, value, 0).astype(value.dtype)
    return lax.psum(kept, axis)


def hann_window(length):
    times = jnp.arange(length, dtype=jnp.int32).astype(jnp.float32)
    return 0.5 - 0.5 * jnp.cos(2.0 * math.pi / length * times)


def forward_table(length, bins):
    times = jnp.arange(length, dtype=jnp.int32)[:, None]
    freqs = jnp.arange(1, bins + 1, dtype=jnp.int32)[None, :]
    phase = 2.0 * math.pi / length * jnp.mod(times * freqs, length).astype(jnp.float32)
    return jnp.concatenate([jnp.cos(phase), -jnp.sin(phase)], axis=1).astype(jnp.bfloat16)


def inverse_table(length, bins, lags):
    freqs = jnp.arange(1, bins + 1, dtype=jnp.int32)[:, None]
    shifts = jnp.arange(lags, dtype=jnp.int32)[None, :] - lags // 2
    phase = 2.0 * math.pi / length * jnp.mod(freqs * shifts, length).astype(jnp.float32)
    return jnp.stack([jnp.cos(phase), -jnp.sin(phase)])


def band_matrix(bins):
    rows = jnp.arange(bins, dtype=jnp.int32)[:, None]
    cols = jnp.arange(bins, dtype=jnp.int32)[None, :]
    near = (jnp.abs(rows - cols) <= HALF_SMOOTH).astype(jnp.float32)
    return near / jnp.sum(near, axis=1, keepdims=True)


def transform(samples):
    length = samples.shape[1]
    bins = length // 2
    wide_data = samples.astype(jnp.float32)
    centered = wide_data - jnp.mean(wide_data, axis=1, keepdims=True)
    tapered = (centered * hann_window(length)[None, :, None]).astype(jnp.bfloat16)
    spectrum = jnp.einsum(
        "wtc,tg->wgc", tapered, forward_table(length, bins), preferred_element_type=jnp.float32
    )
    spectrum = spectrum.reshape(spectrum.shape[0], 2, bins, spectrum.shape[2])
    magnitude = jnp.sqrt(spectrum[:, 0] * spectrum[:, 0] + spectrum[:, 1] * spectrum[:, 1])
    smooth = jnp.einsum(
        "fg,wgc->wfc", band_matrix(bins), magnitude, precision=lax.Precision.HIGHEST
    )
    level = jnp.mean(magnitude, axis=1, keepdims=True)
    scaled = spectrum / (smooth + LEVEL_SHARE * level + EPSILON)[:, None]
    return scaled.astype(jnp.bfloat16)


def paired_source(source):
    real_part = source[:, 0]
    imag_part = source[:, 1]
    first = jnp.concatenate([real_part, -imag_part], axis=2)
    second = jnp.concatenate([imag_part, real_part], axis=2)
    return jnp.stack([first, second], axis=1)


def cross_terms(source, receiver):
    return jnp.einsum(
        "wkfs,wkfc->fsc", paired_source(source), receiver, preferred_element_type=jnp.float32
    )


def to_lags(table, cross):
    bins, doubled, columns = cross.shape
    split = cross.reshape(bins, 2, doubled // 2, columns)
    return jnp.einsum("kfl,fksc->lsc", table, split, precision=lax.Precision.HIGHEST)


def stacks_by_block(table, source, receiver):
    parts = []
    for number in range(NBLK):
        block = lax.slice_in_dim(source, number * SRC, (number + 1) * SRC, axis=3)
        parts.append(to_lags(table, cross_terms(block, receiver)))
    return jnp.concatenate(parts, axis=1)


def on_device(record, valid, sources):
    wide_count = lax.axis_size("wide")
    rep_count = lax.axis_size("rep")
    masked = record * valid.astype(jnp.bfloat16)[:, None, :]
    local_windows, length, channels = masked.shape
    bins = length // 2
    shard = channels // wide_count
    divided = masked.reshape(local_windows, length, wide_count, shard)
    arrived = lax.all_to_all(divided, "wide", split_axis=2, concat_axis=0, tiled=True)
    spectra = transform(arrived.reshape(arrived.shape[0], length, arrived.shape[3]))
    total_windows = spectra.shape[0] * rep_count
    table = inverse_table(length, bins, LAGS) * (1.0 / math.sqrt(total_windows * bins))
    per_shard = shard // SRC
    blocks = []
    for number in range(NBLK):
        block_index = sources[number]
        offset = block_index % per_shard * SRC
        local_block = lax.dynamic_slice_in_dim(spectra, offset, SRC, 3)
        blocks.append(broadcast(local_block, "wide", block_index // per_shard))
    complete = stacks_by_block(table, jnp.concatenate(blocks, axis=3), spectra)
    return lax.psum_scatter(complete, "rep", scatter_dimension=0, tiled=True)


def solution(mesh):
    return jax.shard_map(
        on_device,
        mesh=mesh,
        in_specs=(P(("wide", "rep"), None, None), P(("wide", "rep"), None), P()),
        out_specs=P("rep", None, "wide"),
        check_vma=False,
    )
```

profile of v0, /device:TPU:2, one launch (start us, length us, event | category | flops | bytes accessed | tf_op | source)
XLA Modules:
  0.0 2274.2 jit_solution(2077587218461118139)
XLA Ops:
  7.4 6.4 copy.33
  13.8 4.2 broadcast_multiply_fusion
  18.0 6.5 copy.34
  24.4 4.7 all-to-all-start
  38.5 38.0 %all-to-all-done = bf16[1,256,8,1024]{3,1,0,2:T(8,128)(2,1)} async-done(((bf16[1,256,8,1024]{3,1,0,2:T(8,128)(2,1)}), bf16[1,256,8,1024]{3,1,0,2:T(8,128)(2,1)}, u32[]{:S(2)}, u32[]{:S(2)}) %all-to-all-start) | async-done | bytes 4194336 | tf_op jit(solution)/shard_map/all_to_all | solution.py:104
  76.5 3.1 fusion.15
  79.6 3.6 fusion.20
  83.2 4.6 fusion.80
  89.1 5.3 copy.49
  94.5 5.3 copy.50
  99.8 5.2 fusion.31
  105.8 5.9 add_bitcast_fusion
  111.7 5.5 copy.37
  117.2 10.1 fusion.19
  131.5 59.4 %all-reduce.3.cloned.1.call-done = (bf16[8,2,128,64]{3,0,2,1:T(8,128)(2,1)}, bf16[8,2,128,64]{3,0,2,1:T(8,128)(2,1)}, bf16[8,2,128,64]{3,0,2,1:T(8,128)(2,1)}) async-done(((bf16[8,2,128,64]{3,0,2,1:T(8,128)(2,1)}, bf16[8,2,128,64]{3,0,2,1:T(8,128)(2,1)}, bf16[8,2,128,64]{3,0,2,1:T(8,128)(2,1)}), (bf16[8,2,128,64]{3,0,2,1:T(8,128)(2,1)}, bf16[8,2,128,64]{3,0,2,1:T(8,128)(2,1)}, ...) | async-done | bytes 786448 | tf_op jit(solution)/shard_map/psum | solution.py:20
  195.9 23.1 %fusion.25 = f32[128,128,1024,1]{2,1,3,0:T(8,128)} fusion(bf16[8,2,128,1024]{3,0,2,1:T(8,128)(2,1)S(1)} %copy-done.1, bf16[8,1,128,128]{3,0,1,2:T(8,128)(2,1)S(1)} %get-tuple-element.20, bf16[8,1,128,128]{3,0,1,2:T(8,128)(2,1)S(1)} %get-tuple-element.19), kind=kOutput, calls=%fused_computation.22 | convolution fusion | flops 537133056 | bytes 71827456 | tf_op jit(solution)/shard_map/wkfs,wkfc->fsc/dot_general | solution.py:77
  219.4 24.0 %fusion.35 = f32[128,128,1024,1]{2,1,0,3:T(8,128)} fusion(bf16[8,2,128,1024]{3,0,2,1:T(8,128)(2,1)S(1)} %copy-done.1, bf16[8,1,128,128]{3,0,2,1:T(8,128)(2,1)S(1)} %get-tuple-element.22, bf16[8,1,128,128]{3,0,2,1:T(8,128)(2,1)S(1)} %get-tuple-element.21), kind=kOutput, calls=%fused_computation.33 | convolution fusion | flops 537133056 | bytes 71827456 | tf_op jit(solution)/shard_map/wkfs,wkfc->fsc/dot_general | solution.py:77
  243.3 91.0 %fusion.6 = f32[128,64,1024]{2,0,1:T(8,128)} fusion(f32[128,2,64,1024]{3,2,1,0:T(8,128)} %bitcast.21, f32[1,128,128]{1,2,0:T(8,128)S(1)} %get-tuple-element.26, f32[1,128,128]{1,2,0:T(8,128)S(1)} %get-tuple-element.25), kind=kOutput, calls=%fused_computation.7 | convolution fusion | flops 25769869312 | bytes 100794368 | tf_op jit(solution)/shard_map/kfl,fksc->lsc/dot_general | solution.py:85
  334.4 90.8 %fusion.9 = f32[128,64,1024]{2,0,1:T(8,128)} fusion(f32[128,2,64,1024]{3,2,1,0:T(8,128)} %bitcast.30, f32[1,128,128]{1,2,0:T(8,128)S(1)} %get-tuple-element.26, f32[1,128,128]{1,2,0:T(8,128)S(1)} %get-tuple-element.25), kind=kOutput, calls=%fused_computation.8 | convolution fusion | flops 25769869312 | bytes 100794368 | tf_op jit(solution)/shard_map/kfl,fksc->lsc/dot_general | solution.py:85
  425.4 24.0 %fusion.39 = f32[128,128,1024,1]{2,1,0,3:T(8,128)} fusion(bf16[8,2,128,1024]{3,0,2,1:T(8,128)(2,1)S(1)} %copy-done.1, bf16[8,1,128,128]{3,0,2,1:T(8,128)(2,1)S(1)} %get-tuple-element.24, bf16[8,1,128,128]{3,0,2,1:T(8,128)(2,1)S(1)} %get-tuple-element.23), kind=kOutput, calls=%fused_computation.37 | convolution fusion | flops 537133056 | bytes 71827456 | tf_op jit(solution)/shard_map/wkfs,wkfc->fsc/dot_general | solution.py:77
  449.4 90.8 %fusion.12 = f32[128,64,1024]{2,0,1:T(8,128)} fusion(f32[128,2,64,1024]{3,2,1,0:T(8,128)} %bitcast.39, f32[1,128,128]{1,2,0:T(8,128)S(1)} %get-tuple-element.26, f32[1,128,128]{1,2,0:T(8,128)S(1)} %get-tuple-element.25), kind=kOutput, calls=%fused_computation.9 | convolution fusion | flops 25769869312 | bytes 100794368 | tf_op jit(solution)/shard_map/kfl,fksc->lsc/dot_general | solution.py:85
  540.3 67.3 %pad_maximum_fusion = f32[128,192,1024]{2,0,1:T(8,128)} fusion(f32[128,64,1024]{2,0,1:T(8,128)} %fusion.12, f32[128,64,1024]{2,0,1:T(8,128)} %fusion.9, f32[128,64,1024]{2,0,1:T(8,128)} %fusion.6), kind=kLoop, calls=%fused_computation | loop fusion | flops 50331648 | bytes 201326592 | tf_op jit(solution)/shard_map/concatenate | solution.py:93
  607.6 1634.3 %reduce-scatter.2.cloned.1.call-done = f32[32,192,1024]{2,0,1:T(8,128)} async-done(((f32[128,192,1024]{2,0,1:T(8,128)}), f32[32,192,1024]{2,0,1:T(8,128)}) %reduce-scatter.2.cloned.1.call-update) | async-done | bytes 25165840 | tf_op jit(solution)/shard_map/reduce_scatter | solution.py:116
  2241.9 25.1 %copy.44 = f32[32,192,1024]{2,1,0:T(8,128)} copy(f32[32,192,1024]{2,0,1:T(8,128)} %reduce-scatter.2.cloned.1.call-done) | data formatting | bytes 50331648 | tf_op jit(solution)/shard_map/reduce_scatter | solution.py:116
  (34 shorter events, 14.2 us)
Async XLA Ops:
  24.4 4.7 copy-start.5
  24.4 52.1 %all-to-all-start = ((bf16[1,256,8,1024]{3,1,0,2:T(8,128)(2,1)}), bf16[1,256,8,1024]{3,1,0,2:T(8,128)(2,1)}, u32[]{:S(2)}, u32[]{:S(2)}) async-start(bf16[1,256,8,1024]{3,1,0,2:T(8,128)(2,1)} %copy.34), calls=%async_computation | async-start | bytes 8388608 | tf_op jit(solution)/shard_map/all_to_all | solution.py:104
  29.1 161.7 %all-reduce.3.cloned.1.call-start = ((), (), s32[]{:S(2)}) async-start(), calls=%async_computation.3 | async-start | bytes 3145728 | tf_op jit(solution)/shard_map/psum | solution.py:20
  83.2 5.9 copy-start.2
  99.8 5.2 copy-start.3
  99.8 5.9 copy-start.4
  127.3 2.0 copy-start
  131.1 2110.8 %reduce-scatter.2.cloned.1.call-start = ((), (), s32[]{:S(2)}) async-start(), calls=%async_computation.2 | async-start | bytes 125829120 | tf_op jit(solution)/shard_map/reduce_scatter | solution.py:116
  190.8 5.1 copy-start.1
Sparse Core Ops, SparseCore 0:
  131.2 59.6 all-reduce.2
  607.7 1634.1 reduce-scatter.1
where the time goes:
time: 2280 us; the launch traced here: 2270 us
  waiting for transfers between devices  1730 us (76%)
  matrix products  353 us (15%)
  other arithmetic  96.7 us (4%)
  local copies, waits for them, and re-layouts  65.9 us (3%)
    reduce_scatter x1, waiting for transfers between devices, on_device(): return lax.psum_scatter(complete, 'rep', scatter_dimension=0, tiled=True)  1630 us
    dot_general x3, matrix products, to_lags(): jnp.einsum('kfl,fksc->lsc', table, split, precision=lax.Precision.HIGHEST)  273 us
    dot_general x3, matrix products, cross_terms(): jnp.einsum('wkfs,wkfc->fsc', paired_source(source), receiver, preferred_e...  71.1 us
    concatenate x1, other arithmetic, stacks_by_block(): return jnp.concatenate(parts, axis=1)  67.3 us
    psum x1, waiting for transfers between devices, broadcast(): return lax.psum(kept, axis)  59.4 us
  transfers between devices with their start and end apart: 3, of which 3 were waited for; matrix products, arithmetic and copies ran while one was open for 0% of the time, Pallas kernels for 0%

commit v1 on v0

v1 whole, which is shorter than its diff:
```python
import functools
import math

import jax
import jax.numpy as jnp
import numpy as np
from jax import lax
from jax.experimental import pallas as pl
from jax.experimental.pallas import tpu as pltpu
from jax.sharding import PartitionSpec as P

SRC = 64
LAGS = 128
HALF_SMOOTH = 5
EPSILON = 1e-05
LEVEL_SHARE = 0.2

VMEM_LIMIT = 56 * 1024 * 1024
TILE_LAGS = 2


def forward_table(length, bins):
    phase = 2.0 * math.pi / length * np.mod(np.outer(np.arange(1, bins + 1), np.arange(length)), length)
    return jnp.asarray(np.concatenate([np.cos(phase), -np.sin(phase)], axis=0), jnp.bfloat16)


def hann_window(length):
    return jnp.asarray(0.5 - 0.5 * np.cos(2.0 * math.pi / length * np.arange(length)), jnp.float32)[:, None]


def band_matrix(bins):
    rows = np.arange(bins)
    near = (np.abs(rows[:, None] - rows[None, :]) <= HALF_SMOOTH).astype(np.float32)
    return jnp.asarray(near, jnp.bfloat16), jnp.asarray(1.0 / near.sum(axis=1, keepdims=True), jnp.float32)


def rotation_tables(length, bins, total_windows):
    shifts = np.arange(LAGS) - LAGS // 2
    phase = 2.0 * math.pi / length * np.mod(np.outer(shifts, np.arange(1, bins + 1)), length)
    scale = 1.0 / math.sqrt(total_windows * bins)
    cos, sin = np.cos(phase) * scale, np.sin(phase) * scale
    return jnp.asarray(np.stack([np.concatenate([cos, cos], 1), np.concatenate([sin, sin], 1)], 1), jnp.float32)


def whiten_kernel(record_ref, valid_ref, table_ref, taper_ref, band_ref, inverse_count_ref, out_ref):
    bins = band_ref.shape[0]
    samples = record_ref[...].astype(jnp.float32)
    centered = samples - jnp.mean(samples, axis=0, keepdims=True)
    tapered = (centered * taper_ref[...]).astype(jnp.bfloat16)
    spectrum = jnp.dot(table_ref[...], tapered, preferred_element_type=jnp.float32)
    real, imag = spectrum[:bins], spectrum[bins:]
    magnitude = jnp.sqrt(real * real + imag * imag)
    band = band_ref[...]
    smooth = jnp.zeros_like(magnitude)
    rest = magnitude
    for _ in range(3):
        piece = rest.astype(jnp.bfloat16)
        rest = rest - piece.astype(jnp.float32)
        smooth = smooth + jnp.dot(band, piece, preferred_element_type=jnp.float32)
    smooth = smooth * inverse_count_ref[...]
    level = jnp.mean(magnitude, axis=0, keepdims=True)
    gain = valid_ref[...].astype(jnp.float32) / (smooth + (LEVEL_SHARE * level + EPSILON))
    out_ref[:bins] = (real * gain).astype(jnp.bfloat16)
    out_ref[bins:] = (imag * gain).astype(jnp.bfloat16)


def whiten(record, valid, wide_count):
    length, channels = record.shape
    bins = length // 2
    shard = channels // wide_count
    tile = min(512, shard)
    per = shard // tile
    band, inverse_count = band_matrix(bins)
    fixed = lambda i: (0, 0)
    return pl.pallas_call(
        whiten_kernel,
        grid=(channels // tile,),
        in_specs=[
            pl.BlockSpec((length, tile), lambda i: (0, i)),
            pl.BlockSpec((1, tile), lambda i: (0, i)),
            pl.BlockSpec((2 * bins, length), fixed),
            pl.BlockSpec((length, 1), fixed),
            pl.BlockSpec((bins, bins), fixed),
            pl.BlockSpec((bins, 1), fixed),
        ],
        out_specs=pl.BlockSpec((None, 2 * bins, tile), lambda i: (i // per, 0, i % per)),
        out_shape=jax.ShapeDtypeStruct((wide_count, 2 * bins, shard), jnp.bfloat16),
        compiler_params=pltpu.CompilerParams(vmem_limit_bytes=VMEM_LIMIT),
        name="whiten",
    )(record, valid, forward_table(length, bins), hann_window(length), band, inverse_count)


def rotate_split(source_ref, rotation_ref, high_ref, low_ref):
    windows, rows, depth = source_ref.shape
    for window in range(windows):
        source = source_ref[window].astype(jnp.float32)
        real, imag = source[:, : depth // 2], source[:, depth // 2 :]
        turned = jnp.concatenate([imag, -real], axis=1)
        for lag in range(rotation_ref.shape[0]):
            value = source * rotation_ref[lag, 0:1] + turned * rotation_ref[lag, 1:2]
            high = value.astype(jnp.bfloat16)
            at = (slice(lag * rows, (lag + 1) * rows), slice(window * depth, (window + 1) * depth))
            high_ref[at] = high
            low_ref[at] = (value - high.astype(jnp.float32)).astype(jnp.bfloat16)


def stack_kernel(source_ref, rotation_ref, receiver_ref, *rest):
    out_ref, high_ref, low_ref = rest[-3:]
    before_ref = rest[0] if len(rest) == 4 else None
    rotate_split(source_ref, rotation_ref, high_ref, low_ref)
    lags, rows, channels = out_ref.shape
    tile = min(256, channels)

    @pl.loop(0, channels // tile)
    def _(number):
        columns = pl.ds(pl.multiple_of(number * tile, tile), tile)
        receiver = receiver_ref[:, columns]
        total = jnp.dot(high_ref[...], receiver, preferred_element_type=jnp.float32)
        total = total + jnp.dot(low_ref[...], receiver, preferred_element_type=jnp.float32)
        total = total.reshape(lags, rows, tile)
        if before_ref is not None:
            total = total + before_ref[:, :, columns]
        out_ref[:, :, columns] = total


def add_stacks(source, rotation, receiver, before):
    windows, rows, depth = source.shape
    channels = receiver.shape[2]
    lags = rotation.shape[0]
    receiver = receiver.reshape(windows * depth, channels)
    block = pl.BlockSpec((TILE_LAGS, rows, channels), lambda i: (i, 0, 0))
    operands = [source, rotation, receiver]
    in_specs = [
        pl.BlockSpec((windows, rows, depth), lambda i: (0, 0, 0)),
        pl.BlockSpec((TILE_LAGS, 2, depth), lambda i: (i, 0, 0)),
        pl.BlockSpec((windows * depth, channels), lambda i: (0, 0)),
    ]
    if before is not None:
        operands.append(before)
        in_specs.append(block)
    flops = 4 * lags * rows * windows * depth * channels
    return pl.pallas_call(
        stack_kernel,
        grid=(lags // TILE_LAGS,),
        in_specs=in_specs,
        out_specs=block,
        out_shape=jax.ShapeDtypeStruct((lags, rows, channels), jnp.float32),
        scratch_shapes=[pltpu.VMEM((TILE_LAGS * rows, windows * depth), jnp.bfloat16)] * 2,
        input_output_aliases={} if before is None else {3: 0},
        compiler_params=pltpu.CompilerParams(vmem_limit_bytes=VMEM_LIMIT),
        cost_estimate=pl.CostEstimate(flops=flops, bytes_accessed=lags * rows * channels * 8, transcendentals=0),
        name="add_stacks",
    )(*operands)


def on_device(record, valid, sources):
    wide_count = lax.axis_size("wide")
    rep_count = lax.axis_size("rep")
    rep = lax.axis_index("rep")
    _, length, channels = record.shape
    bins = length // 2
    shard = channels // wide_count
    total_windows = wide_count * rep_count
    lags = LAGS // rep_count
    whitened = whiten(record[0], valid, wide_count)
    per_shard = shard // SRC
    picked = []
    for number in range(sources.shape[0]):
        block = sources[number]
        start = (block // per_shard, 0, block % per_shard * SRC)
        picked.append(lax.dynamic_slice(whitened, start, (1, length, SRC))[0])
    own_source = jnp.concatenate(picked, axis=1).T
    source = lax.all_gather(own_source, "rep")
    source = lax.all_gather(source, "wide", axis=1)
    receiver = lax.all_to_all(whitened, "wide", split_axis=0, concat_axis=0, tiled=True)
    rotation = lax.dynamic_slice_in_dim(rotation_tables(length, bins, total_windows), rep * lags, lags, 0)
    ring = [(i, (i + 1) % rep_count) for i in range(rep_count)]
    stacks = None
    for step in range(rep_count):
        later = lax.ppermute(receiver, "rep", ring) if step < rep_count - 1 else None
        owner = lax.rem(rep + rep_count - step, rep_count)
        here = lax.dynamic_index_in_dim(source, owner, 0, keepdims=False)
        for first in range(0, wide_count, 8):
            part = slice(first, min(first + 8, wide_count))
            stacks = add_stacks(here[part], rotation, receiver[part], stacks)
        receiver = later
    return stacks


def solution(mesh):
    return jax.shard_map(
        on_device,
        mesh=mesh,
        in_specs=(P(("wide", "rep"), None, None), P(("wide", "rep"), None), P()),
        out_specs=P("rep", None, "wide"),
        check_vma=False,
    )
```

time: 2280 us -> 483 us (0.21)
  waiting for transfers between devices: 1730 us -> 95.1 us
  matrix products: 353 us -> 0 us
  Pallas kernels: 0 us -> 334 us
  other arithmetic: 96.7 us -> 0.01 us
  local copies, waits for them, and re-layouts: 65.9 us -> 9.75 us
    reduce_scatter x1 -> x0, waiting for transfers between devices: 1630 us -> none  [on_device(): return lax.psum_scatter(complete, 'rep', scatter_dimension=0, tiled=True)]
    dot_general x8 -> x0, matrix products: 353 us -> none  [the longest x3 273 us: to_lags(): jnp.einsum('kfl,fksc->lsc', table, split, precision=lax.Precision.HIGHEST)]
    pallas_call x0 -> x5, Pallas kernels: none -> 334 us  [the longest x4 318 us: add_stacks(): pl.pallas_call(stack_kernel, grid=(lags // TILE_LAGS,), in_specs=in_specs...]
    concatenate x1 -> x0, other arithmetic: 67.3 us -> none  [stacks_by_block(): return jnp.concatenate(parts, axis=1)]
    psum x1 -> x0, waiting for transfers between devices: 59.4 us -> none  [broadcast(): return lax.psum(kept, axis)]
    ppermute x0 -> x3, waiting for transfers between devices: none -> 36.2 us  [on_device(): lax.ppermute(receiver, 'rep', ring)]
    reduce_scatter x1 -> x0, local copies, waits for them, and re-layouts: 25.1 us -> none  [on_device(): return lax.psum_scatter(complete, 'rep', scatter_dimension=0, tiled=True)]
  transfers between devices with their start and end apart: 3 -> 5, of which waited for: 3 -> 4; matrix products, arithmetic and copies ran while one was open for 0% -> 1% of each run, Pallas kernels for 0% -> 49%
where the time goes in v1:
time: 483 us; the launch traced here: 482 us
  Pallas kernels  334 us (69%)
  waiting for transfers between devices  95.1 us (20%)
  between operations  21.1 us (4%)
  blocking collectives  15.3 us (3%)
  local copies, waits for them, and re-layouts  9.75 us (2%)
  starting transfers between devices  7.26 us (2%)
    pallas_call x4, Pallas kernels, add_stacks(): pl.pallas_call(stack_kernel, grid=(lags // TILE_LAGS,), in_specs=in_specs...  318 us
    all_to_all x1, waiting for transfers between devices, on_device(): lax.all_to_all(whitened, 'wide', split_axis=0, concat_axis=0, tiled=True)  58.9 us
    ppermute x3, waiting for transfers between devices, on_device(): lax.ppermute(receiver, 'rep', ring)  36.2 us
    pallas_call x1, Pallas kernels, whiten(): pl.pallas_call(whiten_kernel, grid=(channels // tile,), in_specs=[pl.Bloc...  15.7 us
    all_gather x1, blocking collectives, on_device(): source = lax.all_gather(own_source, 'rep')  15.3 us
  transfers between devices with their start and end apart: 5, of which 4 were waited for; matrix products, arithmetic and copies ran while one was open for 1% of the time, Pallas kernels for 49%

profile of v1, /device:TPU:2, one launch (start us, length us, event | category | flops | bytes accessed | tf_op | source)
XLA Modules:
  0.0 482.3 jit_solution(1231211589366653679)
XLA Ops:
  6.5 0.0 all-gather.4.cloned.1.call-start
  6.5 1.4 fusion
  15.7 15.7 %whiten.1 = bf16[8,256,1024]{2,1,0:T(8,128)(2,1)} custom-call(bf16[256,8192]{1,0:T(8,128)(2,1)} %bitcast.23, s32[1,8192]{1,0:T(1,128)} %valid_ref.1, bf16[256,256]{1,0:T(8,128)(2,1)} %constant.105.clone.table_ref, f32[256,1]{1,0:T(8,128)} %constant.110.taper_ref, bf16[128,128]{1,0:T(8,128)(2,1)} %constant.103.clone.band_ref, ...), custom_call_target="tpu_custom_call" | custom-call | tf_op jit(solution)/shard_map/whiten/pallas_call | solution.py:75
  31.4 1.0 constant_dynamic-slice_fusion.3
  32.4 0.1 copy.12
  32.5 0.1 copy.13
  32.6 0.1 copy.14
  32.7 15.3 %all-gather = bf16[768,256]{1,0:T(8,128)(2,1)} all-gather(bf16[192,256]{1,0:T(8,128)(2,1)S(1)} %maximum_bitcast_fusion), channel_id=2, replica_groups=mesh['wide'=8,'rep'=4] {'rep'}, dimensions={0}, use_global_device_ids=true | all-gather | bytes 491520 | tf_op jit(solution)/shard_map/all_gather | solution.py:173
  48.0 0.0 all-gather.4.cloned.1.call-update
  48.1 5.0 %all-to-all-start = ((bf16[8,256,1024]{2,1,0:T(8,128)(2,1)}), bf16[8,256,1024]{2,1,0:T(8,128)(2,1)}, u32[]{:S(2)}, u32[]{:S(2)}) async-start(bf16[8,256,1024]{2,1,0:T(8,128)(2,1)} %whiten.1), calls=%async_computation | async-start | bytes 8388608 | tf_op jit(solution)/shard_map/all_to_all | solution.py:175
  53.0 1.5 constant_dynamic-slice_fusion.rotation_ref
  54.5 58.9 %all-to-all-done = bf16[8,256,1024]{2,1,0:T(8,128)(2,1)} async-done(((bf16[8,256,1024]{2,1,0:T(8,128)(2,1)}), bf16[8,256,1024]{2,1,0:T(8,128)(2,1)}, u32[]{:S(2)}, u32[]{:S(2)}) %all-to-all-start) | async-done | bytes 4194336 | tf_op jit(solution)/shard_map/all_to_all | solution.py:175
  113.4 2.3 collective-permute-start
  115.7 3.6 dynamic-slice_bitcast_fusion
  119.3 79.0 %add_stacks.4.rest_0_ = f32[32,192,1024]{2,1,0:T(8,128)} custom-call(bf16[8,192,256]{2,1,0:T(8,128)(2,1)} %get-tuple-element.8.source_ref, f32[32,2,256]{2,1,0:T(2,128)} %constant_dynamic-slice_fusion.rotation_ref, bf16[2048,1024]{1,0:T(8,128)(2,1)} %bitcast.17.receiver_ref), custom_call_target="tpu_custom_call" | custom-call | flops 51539607552 | bytes 50331648 | tf_op jit(solution)/shard_map/add_stacks/pallas_call | solution.py:142
  198.3 10.4 %collective-permute-done = bf16[8,256,1024]{2,1,0:T(8,128)(2,1)} collective-permute-done((bf16[8,256,1024]{2,1,0:T(8,128)(2,1)}, bf16[8,256,1024]{2,1,0:T(8,128)(2,1)}, u32[]{:S(2)}, u32[]{:S(2)}) %collective-permute-start) | collective-permute-done | bytes 4194336 | tf_op jit(solution)/shard_map/ppermute | solution.py:180
  208.7 0.0 collective-permute-start.1
  208.7 79.7 %add_stacks.5.rest_0_ = f32[32,192,1024]{2,1,0:T(8,128)} custom-call(bf16[8,192,256]{2,1,0:T(8,128)(2,1)} %get-tuple-element.9.source_ref, f32[32,2,256]{2,1,0:T(2,128)} %constant_dynamic-slice_fusion.rotation_ref, bf16[2048,1024]{1,0:T(8,128)(2,1)} %bitcast.15.receiver_ref, f32[32,192,1024]{2,1,0:T(8,128)} %add_stacks.4.rest_0_), custom_call_target="tpu_custom_call", output_to_operand_aliasing={{}: (3, {})} | custom-call | flops 51539607552 | bytes 50331648 | tf_op jit(solution)/shard_map/add_stacks/pallas_call | solution.py:142
  288.4 14.3 %collective-permute-done.1 = bf16[8,256,1024]{2,1,0:T(8,128)(2,1)S(1)} collective-permute-done((bf16[8,256,1024]{2,1,0:T(8,128)(2,1)}, bf16[8,256,1024]{2,1,0:T(8,128)(2,1)S(1)}, u32[]{:S(2)}, u32[]{:S(2)}) %collective-permute-start.1) | collective-permute-done | bytes 4194336 | tf_op jit(solution)/shard_map/ppermute | solution.py:180
  302.8 0.0 collective-permute-start.2
  302.8 2.0 copy-done
  304.7 79.7 %add_stacks.6.rest_0_ = f32[32,192,1024]{2,1,0:T(8,128)} custom-call(bf16[8,192,256]{2,1,0:T(8,128)(2,1)} %get-tuple-element.10.source_ref, f32[32,2,256]{2,1,0:T(2,128)} %constant_dynamic-slice_fusion.rotation_ref, bf16[2048,1024]{1,0:T(8,128)(2,1)} %bitcast.29, f32[32,192,1024]{2,1,0:T(8,128)} %add_stacks.5.rest_0_), custom_call_target="tpu_custom_call", output_to_operand_aliasing={{}: (3, {})} | custom-call | flops 51539607552 | bytes 50331648 | tf_op jit(solution)/shard_map/add_stacks/pallas_call | solution.py:142
  384.4 11.4 %collective-permute-done.2 = bf16[8,256,1024]{2,1,0:T(8,128)(2,1)} collective-permute-done((bf16[8,256,1024]{2,1,0:T(8,128)(2,1)S(1)}, bf16[8,256,1024]{2,1,0:T(8,128)(2,1)}, u32[]{:S(2)}, u32[]{:S(2)}) %collective-permute-start.2) | collective-permute-done | bytes 4194336 | tf_op jit(solution)/shard_map/ppermute | solution.py:180
  395.8 79.7 %add_stacks.7 = f32[32,192,1024]{2,1,0:T(8,128)} custom-call(bf16[8,192,256]{2,1,0:T(8,128)(2,1)} %get-tuple-element.11.source_ref, f32[32,2,256]{2,1,0:T(2,128)} %constant_dynamic-slice_fusion.rotation_ref, bf16[2048,1024]{1,0:T(8,128)(2,1)} %bitcast.11.receiver_ref, f32[32,192,1024]{2,1,0:T(8,128)} %add_stacks.6.rest_0_), custom_call_target="tpu_custom_call", output_to_operand_aliasing={{}: (3, {})} | custom-call | flops 51539607552 | bytes 50331648 | tf_op jit(solution)/shard_map/add_stacks/pallas_call | solution.py:142
  (3 shorter events, 0.0 us)
Async XLA Ops:
  6.5 109.2 %all-gather.4.cloned.1.call-start = ((), (), s32[]{:S(2)}) async-start(), calls=%async_computation.1 | async-start | bytes 3538944 | tf_op jit(solution)/shard_map/all_gather | solution.py:174
  48.1 65.3 %all-to-all-start = ((bf16[8,256,1024]{2,1,0:T(8,128)(2,1)}), bf16[8,256,1024]{2,1,0:T(8,128)(2,1)}, u32[]{:S(2)}, u32[]{:S(2)}) async-start(bf16[8,256,1024]{2,1,0:T(8,128)(2,1)} %whiten.1), calls=%async_computation | async-start | bytes 8388608 | tf_op jit(solution)/shard_map/all_to_all | solution.py:175
  113.4 95.3 %collective-permute-start = (bf16[8,256,1024]{2,1,0:T(8,128)(2,1)}, bf16[8,256,1024]{2,1,0:T(8,128)(2,1)}, u32[]{:S(2)}, u32[]{:S(2)}) collective-permute-start(bf16[8,256,1024]{2,1,0:T(8,128)(2,1)} %all-to-all-done), channel_id=1, source_target_pairs={{0,1},{1,2},{2,3},{3,0},{4,5},{5,6},{6,7},{7,4},{8,9},{9,10},{10,1... | collective-permute-start | bytes 12582920 | tf_op jit(solution)/shard_map/ppermute | solution.py:180
  208.7 94.0 %collective-permute-start.1 = (bf16[8,256,1024]{2,1,0:T(8,128)(2,1)}, bf16[8,256,1024]{2,1,0:T(8,128)(2,1)S(1)}, u32[]{:S(2)}, u32[]{:S(2)}) collective-permute-start(bf16[8,256,1024]{2,1,0:T(8,128)(2,1)} %collective-permute-done), channel_id=1, source_target_pairs={{0,1},{1,2},{2,3},{3,0},{4,5},{5,6},{6,7},{7,4},{8,9},{9,10},{10,1... | collective-permute-start | bytes 12582920 | tf_op jit(solution)/shard_map/ppermute | solution.py:180
  302.8 2.0 copy-start
  302.8 93.0 %collective-permute-start.2 = (bf16[8,256,1024]{2,1,0:T(8,128)(2,1)S(1)}, bf16[8,256,1024]{2,1,0:T(8,128)(2,1)}, u32[]{:S(2)}, u32[]{:S(2)}) collective-permute-start(bf16[8,256,1024]{2,1,0:T(8,128)(2,1)S(1)} %collective-permute-done.1), channel_id=1, source_target_pairs={{0,1},{1,2},{2,3},{3,0},{4,5},{5,6},{6,7},{7,4},{8,9},{9,10},{10,1... | collective-permute-start | bytes 12582920 | tf_op jit(solution)/shard_map/ppermute | solution.py:180
Sparse Core Ops, SparseCore 0:
  48.2 64.1 all-gather.3

commit v2 on v1

v2 whole, which is shorter than its diff:
```python
import functools
import functools
import math

import jax
import jax.numpy as jnp
import numpy as np
from jax import lax
from jax.experimental import pallas as pl
from jax.experimental.pallas import tpu as pltpu
from jax.sharding import PartitionSpec as P

SRC = 64
LAGS = 128
HALF_SMOOTH = 5
EPSILON = 1e-05
LEVEL_SHARE = 0.2

VMEM_LIMIT = 56 * 1024 * 1024
PAIR = 2


def forward_table(length, bins):
    phase = 2.0 * math.pi / length * np.mod(np.outer(np.arange(1, bins + 1), np.arange(length)), length)
    return jnp.asarray(np.concatenate([np.cos(phase), -np.sin(phase)], axis=0), jnp.bfloat16)


def hann_window(length):
    return jnp.asarray(0.5 - 0.5 * np.cos(2.0 * math.pi / length * np.arange(length)), jnp.float32)[:, None]


def band_matrix(bins):
    rows = np.arange(bins)
    near = (np.abs(rows[:, None] - rows[None, :]) <= HALF_SMOOTH).astype(np.float32)
    return jnp.asarray(near, jnp.bfloat16), jnp.asarray(1.0 / near.sum(axis=1, keepdims=True), jnp.float32)


def rotation_tables(length, bins, total_windows):
    shifts = np.arange(LAGS) - LAGS // 2
    phase = 2.0 * math.pi / length * np.mod(np.outer(shifts, np.arange(1, bins + 1)), length)
    scale = 1.0 / math.sqrt(total_windows * bins)
    cos, sin = np.cos(phase) * scale, np.sin(phase) * scale
    return jnp.asarray(np.stack([np.concatenate([cos, cos], 1), np.concatenate([sin, sin], 1)], 1), jnp.float32)


def whiten_kernel(record_ref, valid_ref, table_ref, taper_ref, band_ref, inverse_count_ref, out_ref):
    bins = band_ref.shape[0]
    samples = record_ref[...].astype(jnp.float32)
    centered = samples - jnp.mean(samples, axis=0, keepdims=True)
    tapered = (centered * taper_ref[...]).astype(jnp.bfloat16)
    spectrum = jnp.dot(table_ref[...], tapered, preferred_element_type=jnp.float32)
    real, imag = spectrum[:bins], spectrum[bins:]
    magnitude = jnp.sqrt(real * real + imag * imag)
    band = band_ref[...]
    smooth = jnp.zeros_like(magnitude)
    rest = magnitude
    for _ in range(3):
        piece = rest.astype(jnp.bfloat16)
        rest = rest - piece.astype(jnp.float32)
        smooth = smooth + jnp.dot(band, piece, preferred_element_type=jnp.float32)
    smooth = smooth * inverse_count_ref[...]
    level = jnp.mean(magnitude, axis=0, keepdims=True)
    gain = valid_ref[...].astype(jnp.float32) / (smooth + (LEVEL_SHARE * level + EPSILON))
    out_ref[:bins] = (real * gain).astype(jnp.bfloat16)
    out_ref[bins:] = (imag * gain).astype(jnp.bfloat16)


def whiten(record, valid, wide_count, parts, part):
    length, channels = record.shape
    bins = length // 2
    shard = channels // wide_count
    width = shard // parts
    tile = min(512, width)
    per_shard, per = shard // tile, width // tile
    band, inverse_count = band_matrix(bins)
    fixed = lambda i, j: (0, 0)
    columns = lambda i, j: (0, i * per_shard + part * per + j)
    return pl.pallas_call(
        whiten_kernel,
        grid=(wide_count, per),
        in_specs=[
            pl.BlockSpec((length, tile), columns),
            pl.BlockSpec((1, tile), columns),
            pl.BlockSpec((2 * bins, length), fixed),
            pl.BlockSpec((length, 1), fixed),
            pl.BlockSpec((bins, bins), fixed),
            pl.BlockSpec((bins, 1), fixed),
        ],
        out_specs=pl.BlockSpec((None, 2 * bins, tile), lambda i, j: (i, 0, j)),
        out_shape=jax.ShapeDtypeStruct((wide_count, 2 * bins, width), jnp.bfloat16),
        compiler_params=pltpu.CompilerParams(vmem_limit_bytes=VMEM_LIMIT),
        name="whiten",
    )(record, valid, forward_table(length, bins), hann_window(length), band, inverse_count)


def rotate_split(source_ref, rotation_ref, first_lag, window, split_ref):
    _, rows, depth = source_ref.shape
    source = source_ref[window].astype(jnp.float32)
    turned = jnp.concatenate([source[:, depth // 2 :], -source[:, : depth // 2]], axis=1)
    columns = pl.ds(pl.multiple_of(window * depth, depth), depth)
    for lag in range(PAIR):
        rotation = rotation_ref[first_lag + lag]
        value = source * rotation[0:1] + turned * rotation[1:2]
        high = value.astype(jnp.bfloat16)
        split_ref[lag * rows : (lag + 1) * rows, columns] = high
        low = (value - high.astype(jnp.float32)).astype(jnp.bfloat16)
        split_ref[(PAIR + lag) * rows : (PAIR + lag + 1) * rows, columns] = low


def stack_kernel(fresh, source_ref, rotation_ref, receiver_ref, *rest):
    out_ref, even_ref, odd_ref = rest[-3:]
    before_ref = None if fresh else rest[0]
    step = pl.program_id(0)
    windows = source_ref.shape[0]
    _, rows, channels = out_ref.shape
    total_lags = rotation_ref.shape[0]
    tile = min(256, channels)
    tiles = channels // tile
    share = windows // tiles

    @pl.when(step == 0)
    def _():
        @pl.loop(0, windows)
        def _(window):
            rotate_split(source_ref, rotation_ref, 0, window, even_ref)

    for number, (now_ref, later_ref) in enumerate(((even_ref, odd_ref), (odd_ref, even_ref))):
        next_lag = jnp.minimum((2 * step + number + 1) * PAIR, total_lags - PAIR)
        lags = slice(number * PAIR, (number + 1) * PAIR)

        @pl.loop(0, tiles)
        def _(at):
            for offset in range(share):
                rotate_split(source_ref, rotation_ref, next_lag, at * share + offset, later_ref)
            columns = pl.ds(pl.multiple_of(at * tile, tile), tile)
            both = jnp.dot(now_ref[...], receiver_ref[:, columns], preferred_element_type=jnp.float32)
            total = (both[: PAIR * rows] + both[PAIR * rows :]).reshape(PAIR, rows, tile)
            if before_ref is not None:
                total = total + before_ref[lags, :, columns]
            out_ref[lags, :, columns] = total


def add_stacks(source, rotation, receiver, before, fresh, shard, part):
    windows, rows, depth = source.shape
    channels = receiver.shape[2]
    lags = rotation.shape[0]
    receiver = receiver.reshape(windows * depth, channels)
    block = pl.BlockSpec((2 * PAIR, rows, channels), lambda i: (i, 0, part))
    operands = [source, rotation, receiver]
    in_specs = [
        pl.BlockSpec((windows, rows, depth), lambda i: (0, 0, 0)),
        pl.BlockSpec((lags, 2, depth), lambda i: (0, 0, 0)),
        pl.BlockSpec((windows * depth, channels), lambda i: (0, 0)),
    ]
    if before is not None:
        operands.append(before)
        in_specs.append(pl.BlockSpec(memory_space=pl.ANY) if fresh else block)
    flops = 4 * lags * rows * windows * depth * channels
    return pl.pallas_call(
        functools.partial(stack_kernel, fresh),
        grid=(lags // (2 * PAIR),),
        in_specs=in_specs,
        out_specs=block,
        out_shape=jax.ShapeDtypeStruct((lags, rows, shard), jnp.float32),
        scratch_shapes=[pltpu.VMEM((2 * PAIR * rows, windows * depth), jnp.bfloat16)] * 2,
        input_output_aliases={} if before is None else {3: 0},
        compiler_params=pltpu.CompilerParams(vmem_limit_bytes=VMEM_LIMIT),
        cost_estimate=pl.CostEstimate(flops=flops, bytes_accessed=lags * rows * channels * 8, transcendentals=0),
        name="add_stacks",
    )(*operands)


def pick_sources(whitened, sources):
    length, width = whitened[0].shape[1:]
    per_part = width // SRC
    per_shard = per_part * len(whitened)
    picked = []
    for number in range(sources.shape[0]):
        block = sources[number]
        within = block % per_shard
        start = (block // per_shard, 0, within % per_part * SRC)
        found = [lax.dynamic_slice(one, start, (1, length, SRC))[0] for one in whitened]
        chosen = found[0]
        for part in range(1, len(found)):
            chosen = jnp.where(within // per_part == part, found[part], chosen)
        picked.append(chosen)
    return jnp.concatenate(picked, axis=1).T


def on_device(record, valid, sources):
    wide_count = lax.axis_size("wide")
    rep_count = lax.axis_size("rep")
    rep = lax.axis_index("rep")
    _, length, channels = record.shape
    bins = length // 2
    shard = channels // wide_count
    total_windows = wide_count * rep_count
    lags = LAGS // rep_count
    parts = 2 if shard % 512 == 0 else 1
    whitened = [whiten(record[0], valid, wide_count, parts, part) for part in range(parts)]
    ring = [(i, (i + 1) % rep_count) for i in range(rep_count)]
    pass_on = lambda block: lax.ppermute(block, "rep", ring)
    spread = lambda block: lax.all_to_all(block, "wide", split_axis=0, concat_axis=0, tiled=True)
    source = lax.all_gather(pick_sources(whitened, sources), ("wide", "rep"))
    source = source.reshape(wide_count, rep_count, *source.shape[1:])
    rotation = lax.dynamic_slice_in_dim(rotation_tables(length, bins, total_windows), rep * lags, lags, 0)

    stacks, seen = None, set()

    def add(step, part, receiver):
        nonlocal stacks
        owner = lax.rem(rep + rep_count - step, rep_count)
        here = lax.dynamic_index_in_dim(source, owner, 1, keepdims=False)
        for first in range(0, wide_count, 8):
            chosen = slice(first, min(first + 8, wide_count))
            stacks = add_stacks(here[chosen], rotation, receiver[chosen], stacks, part not in seen, shard, part)
            seen.add(part)

    def after_add(block):
        nonlocal stacks
        block, stacks = lax.optimization_barrier((block, stacks))
        return block

    last = parts - 1
    held = spread(whitened[last])
    waiting = [(0, last, held)]
    if parts == 2:
        travelling = whitened[0]
        for step in range(rep_count):
            if step >= 2:
                add(*waiting.pop(0))
                travelling = after_add(travelling)
            waiting.append((step, 0, spread(travelling)))
            if step < rep_count - 1:
                travelling = pass_on(travelling)
        held, _ = lax.optimization_barrier((held, travelling))
    for step in range(1, rep_count):
        held = pass_on(held)
        if parts == 2 and step < rep_count - 1:
            add(*waiting.pop(0))
            held = after_add(held)
        waiting.append((step, last, held))
    for item in waiting:
        add(*item)
    return stacks


def solution(mesh):
    return jax.shard_map(
        on_device,
        mesh=mesh,
        in_specs=(P(("wide", "rep"), None, None), P(("wide", "rep"), None), P()),
        out_specs=P("rep", None, "wide"),
        check_vma=False,
    )
```

time: 483 us -> 634 us (1.31)
  Pallas kernels: 334 us -> 452 us
  waiting for transfers between devices: 95.1 us -> 118 us
  starting transfers between devices: 7.26 us -> 28.7 us
  blocking collectives: 15.3 us -> 0 us
    pallas_call x5 -> x10, Pallas kernels: 334 us -> 452 us  [the longest x8 435 us: add_stacks(): pl.pallas_call(functools.partial(stack_kernel, fresh), grid=(lags // (2 *...]
    all_gather x1, waiting for transfers between devices: 0.01 us -> 73.8 us  [on_device(): source = lax.all_gather(pick_sources(whitened, sources), ('wide', 'rep'))]
    all_to_all x1 -> x5, waiting for transfers between devices: 58.9 us -> 0.01 us  [on_device(): lax.all_to_all(block, 'wide', split_axis=0, concat_axis=0, tiled=True)]
    all_to_all x1 -> x5, starting transfers between devices: 4.97 us -> 22.1 us  [on_device(): lax.all_to_all(block, 'wide', split_axis=0, concat_axis=0, tiled=True)]
    all_gather x1 -> x0, blocking collectives: 15.3 us -> none  [on_device(): source = lax.all_gather(own_source, 'rep')]
    ppermute x3 -> x6, waiting for transfers between devices: 36.2 us -> 44.3 us  [on_device(): pass_on = lambda block: lax.ppermute(block, 'rep', ring)]
  transfers between devices with their start and end apart: 5 -> 12, of which waited for: 4 -> 2; matrix products, arithmetic and copies ran while one was open for 1% -> 1% of each run, Pallas kernels for 49% -> 60%
where the time goes in v2:
time: 634 us; the launch traced here: 632 us
  Pallas kernels  452 us (71%)
  waiting for transfers between devices  118 us (19%)
  starting transfers between devices  28.7 us (5%)
  between operations  21.4 us (3%)
  local copies, waits for them, and re-layouts  9.93 us (2%)
    pallas_call x8, Pallas kernels, add_stacks(): pl.pallas_call(functools.partial(stack_kernel, fresh), grid=(lags // (2 *...  435 us
    all_gather x1, waiting for transfers between devices, on_device(): source = lax.all_gather(pick_sources(whitened, sources), ('wide', 'rep'))  73.8 us
    ppermute x6, waiting for transfers between devices, on_device(): pass_on = lambda block: lax.ppermute(block, 'rep', ring)  44.3 us
    all_to_all x5, starting transfers between devices, on_device(): lax.all_to_all(block, 'wide', split_axis=0, concat_axis=0, tiled=True)  22.1 us
    pallas_call x2, Pallas kernels, whiten(): pl.pallas_call(whiten_kernel, grid=(wide_count, per), in_specs=[pl.BlockS...  17.2 us
  transfers between devices with their start and end apart: 12, of which 2 were waited for; matrix products, arithmetic and copies ran while one was open for 1% of the time, Pallas kernels for 60%

profile of v2, /device:TPU:2, one launch (start us, length us, event | category | flops | bytes accessed | tf_op | source)
XLA Modules:
  0.0 631.8 jit_solution(9350732962217006900)
XLA Ops:
  6.5 1.4 fusion
  16.0 8.6 %whiten.3 = bf16[8,256,512]{2,1,0:T(8,128)(2,1)} custom-call(bf16[256,8192]{1,0:T(8,128)(2,1)} %bitcast.29, s32[1,8192]{1,0:T(1,128)} %valid_ref.3, bf16[256,256]{1,0:T(8,128)(2,1)} %constant.151.clone.table_ref, f32[256,1]{1,0:T(8,128)} %constant.156.taper_ref, bf16[128,128]{1,0:T(8,128)(2,1)} %constant.149.clone.band_ref, ...), custom_call_target="tpu_custom_call" | custom-call | tf_op jit(solution)/shard_map/whiten/pallas_call | solution.py:78
  24.6 8.6 %whiten.2 = bf16[8,256,512]{2,1,0:T(8,128)(2,1)} custom-call(bf16[256,8192]{1,0:T(8,128)(2,1)} %bitcast.30, s32[1,8192]{1,0:T(1,128)} %valid_ref.3, bf16[256,256]{1,0:T(8,128)(2,1)} %constant.151.clone.table_ref, f32[256,1]{1,0:T(8,128)} %constant.156.taper_ref, bf16[128,128]{1,0:T(8,128)(2,1)} %constant.149.clone.band_ref, ...), custom_call_target="tpu_custom_call" | custom-call | tf_op jit(solution)/shard_map/whiten/pallas_call | solution.py:78
  35.3 1.6 collective-permute-start
  36.9 4.3 all-to-all-start
  41.2 1.5 constant_dynamic-slice_fusion.rotation_ref
  42.6 44.3 %collective-permute-done = bf16[8,256,512]{2,1,0:T(8,128)(2,1)} collective-permute-done((bf16[8,256,512]{2,1,0:T(8,128)(2,1)}, bf16[8,256,512]{2,1,0:T(8,128)(2,1)}, u32[]{:S(2)}, u32[]{:S(2)}) %collective-permute-start) | collective-permute-done | bytes 2097184 | tf_op jit(solution)/shard_map/ppermute | solution.py:202
  87.0 73.8 %all-gather.3.cloned.1.call-done = bf16[6144,256]{1,0:T(8,128)(2,1)} async-done(((bf16[192,256]{1,0:T(8,128)(2,1)}), bf16[6144,256]{1,0:T(8,128)(2,1)}) %all-gather.3.cloned.1.call-update) | async-done | bytes 3145744 | tf_op jit(solution)/shard_map/all_gather | solution.py:204
  160.7 3.6 dynamic-slice_bitcast_fusion
  165.7 4.9 all-to-all-start.1
  170.5 53.9 %add_stacks.8.rest_0_ = f32[32,192,1024]{2,1,0:T(8,128)} custom-call(bf16[8,192,256]{2,1,0:T(8,128)(2,1)} %get-tuple-element.28.source_ref, f32[32,2,256]{2,1,0:T(2,128)} %constant_dynamic-slice_fusion.rotation_ref, bf16[2048,512]{1,0:T(8,128)(2,1)} %bitcast.32), custom_call_target="tpu_custom_call" | custom-call | flops 25769803776 | bytes 25165824 | tf_op jit(solution)/shard_map/add_stacks/pallas_call | solution.py:159
  225.0 4.4 all-to-all-start.2
  229.4 54.1 %add_stacks.9.rest_0_ = f32[32,192,1024]{2,1,0:T(8,128)} custom-call(bf16[8,192,256]{2,1,0:T(8,128)(2,1)} %get-tuple-element.28.source_ref, f32[32,2,256]{2,1,0:T(2,128)} %constant_dynamic-slice_fusion.rotation_ref, bf16[2048,512]{1,0:T(8,128)(2,1)} %bitcast.12.receiver_ref, f32[32,192,1024]{2,1,0:T(8,128)} %add_stacks.8.rest_0_), custom_call_target="tpu_custom_call", output_to_operand_aliasing={{}: (3, {})} | custom-call | flops 25769803776 | bytes 25165824 | tf_op jit(solution)/shard_map/add_stacks/pallas_call | solution.py:159
  284.2 4.4 all-to-all-start.3
  288.6 54.6 %add_stacks.10.rest_0_ = f32[32,192,1024]{2,1,0:T(8,128)} custom-call(bf16[8,192,256]{2,1,0:T(8,128)(2,1)} %get-tuple-element.27.source_ref, f32[32,2,256]{2,1,0:T(2,128)} %constant_dynamic-slice_fusion.rotation_ref, bf16[2048,512]{1,0:T(8,128)(2,1)} %bitcast.14.receiver_ref, f32[32,192,1024]{2,1,0:T(8,128)} %add_stacks.9.rest_0_), custom_call_target="tpu_custom_call", output_to_operand_aliasing={{}: (3, {})} | custom-call | flops 25769803776 | bytes 25165824 | tf_op jit(solution)/shard_map/add_stacks/pallas_call | solution.py:159
  343.1 2.0 collective-permute-start.4
  345.2 4.2 all-to-all-start.4
  349.4 54.6 %add_stacks.11.rest_0_ = f32[32,192,1024]{2,1,0:T(8,128)} custom-call(bf16[8,192,256]{2,1,0:T(8,128)(2,1)} %get-tuple-element.26.source_ref, f32[32,2,256]{2,1,0:T(2,128)} %constant_dynamic-slice_fusion.rotation_ref, bf16[2048,512]{1,0:T(8,128)(2,1)} %bitcast.16.receiver_ref, f32[32,192,1024]{2,1,0:T(8,128)} %add_stacks.10.rest_0_), custom_call_target="tpu_custom_call", output_to_operand_aliasing={{}: (3, {})} | custom-call | flops 25769803776 | bytes 25165824 | tf_op jit(solution)/shard_map/add_stacks/pallas_call | solution.py:159
  404.0 1.7 collective-permute-start.5
  405.7 1.3 copy-done.2
  407.0 54.6 %add_stacks.12.rest_0_ = f32[32,192,1024]{2,1,0:T(8,128)} custom-call(bf16[8,192,256]{2,1,0:T(8,128)(2,1)} %get-tuple-element.29.source_ref, f32[32,2,256]{2,1,0:T(2,128)} %constant_dynamic-slice_fusion.rotation_ref, bf16[2048,512]{1,0:T(8,128)(2,1)} %bitcast.33, f32[32,192,1024]{2,1,0:T(8,128)} %add_stacks.11.rest_0_), custom_call_target="tpu_custom_call", output_to_operand_aliasing={{}: (3, {})} | custom-call | flops 25769803776 | bytes 25165824 | tf_op jit(solution)/shard_map/add_stacks/pallas_call | solution.py:159
  461.6 54.5 %add_stacks.13.rest_0_ = f32[32,192,1024]{2,1,0:T(8,128)} custom-call(bf16[8,192,256]{2,1,0:T(8,128)(2,1)} %get-tuple-element.27.source_ref, f32[32,2,256]{2,1,0:T(2,128)} %constant_dynamic-slice_fusion.rotation_ref, bf16[2048,512]{1,0:T(8,128)(2,1)} %bitcast.19.receiver_ref, f32[32,192,1024]{2,1,0:T(8,128)} %add_stacks.12.rest_0_), custom_call_target="tpu_custom_call", output_to_operand_aliasing={{}: (3, {})} | custom-call | flops 25769803776 | bytes 25165824 | tf_op jit(solution)/shard_map/add_stacks/pallas_call | solution.py:159
  516.0 54.5 %add_stacks.14.rest_0_ = f32[32,192,1024]{2,1,0:T(8,128)} custom-call(bf16[8,192,256]{2,1,0:T(8,128)(2,1)} %get-tuple-element.26.source_ref, f32[32,2,256]{2,1,0:T(2,128)} %constant_dynamic-slice_fusion.rotation_ref, bf16[2048,512]{1,0:T(8,128)(2,1)} %bitcast.18.receiver_ref, f32[32,192,1024]{2,1,0:T(8,128)} %add_stacks.13.rest_0_), custom_call_target="tpu_custom_call", output_to_operand_aliasing={{}: (3, {})} | custom-call | flops 25769803776 | bytes 25165824 | tf_op jit(solution)/shard_map/add_stacks/pallas_call | solution.py:159
  570.5 54.5 %add_stacks.15 = f32[32,192,1024]{2,1,0:T(8,128)} custom-call(bf16[8,192,256]{2,1,0:T(8,128)(2,1)} %get-tuple-element.29.source_ref, f32[32,2,256]{2,1,0:T(2,128)} %constant_dynamic-slice_fusion.rotation_ref, bf16[2048,512]{1,0:T(8,128)(2,1)} %bitcast.17.receiver_ref, f32[32,192,1024]{2,1,0:T(8,128)} %add_stacks.14.rest_0_), custom_call_target="tpu_custom_call", output_to_operand_aliasing={{}: (3, {})} | custom-call | flops 25769803776 | bytes 25165824 | tf_op jit(solution)/shard_map/add_stacks/pallas_call | solution.py:159
  (23 shorter events, 4.7 us)
Async XLA Ops:
  6.5 154.2 %all-gather.3.cloned.1.call-start = ((), (), s32[]{:S(2)}) async-start(), calls=%async_computation.5 | async-start | bytes 3244032 | tf_op jit(solution)/shard_map/all_gather | solution.py:204
  35.3 51.7 %collective-permute-start = (bf16[8,256,512]{2,1,0:T(8,128)(2,1)}, bf16[8,256,512]{2,1,0:T(8,128)(2,1)}, u32[]{:S(2)}, u32[]{:S(2)}) collective-permute-start(bf16[8,256,512]{2,1,0:T(8,128)(2,1)} %whiten.3), channel_id=1, source_target_pairs={{0,1},{1,2},{2,3},{3,0},{4,5},{5,6},{6,7},{7,4},{8,9},{9,10},{10,1... | collective-permute-start | bytes 6291464 | tf_op jit(solution)/shard_map/ppermute | solution.py:202
  36.9 127.4 %all-to-all-start = ((bf16[8,256,512]{2,1,0:T(8,128)(2,1)}), bf16[8,256,512]{2,1,0:T(8,128)(2,1)S(1)}, u32[]{:S(2)}, u32[]{:S(2)}) async-start(bf16[8,256,512]{2,1,0:T(8,128)(2,1)} %whiten.2), calls=%async_computation | async-start | bytes 4194304 | tf_op jit(solution)/shard_map/all_to_all | solution.py:203
  87.0 137.5 %collective-permute-start.1 = (bf16[8,256,512]{2,1,0:T(8,128)(2,1)}, bf16[8,256,512]{2,1,0:T(8,128)(2,1)}, u32[]{:S(2)}, u32[]{:S(2)}) collective-permute-start(bf16[8,256,512]{2,1,0:T(8,128)(2,1)} %collective-permute-done), channel_id=1, source_target_pairs={{0,1},{1,2},{2,3},{3,0},{4,5},{5,6},{6,7},{7,4},{8,9},{9,10},{10,1... | collective-permute-start | bytes 6291464 | tf_op jit(solution)/shard_map/ppermute | solution.py:202
  164.3 1.3 copy-start
  165.7 59.3 %all-to-all-start.1 = ((bf16[8,256,512]{2,1,0:T(8,128)(2,1)}), bf16[8,256,512]{2,1,0:T(8,128)(2,1)}, u32[]{:S(2)}, u32[]{:S(2)}) async-start(bf16[8,256,512]{2,1,0:T(8,128)(2,1)} %whiten.3), calls=%async_computation.1 | async-start | bytes 4194304 | tf_op jit(solution)/shard_map/all_to_all | solution.py:203
  224.5 59.0 %collective-permute-start.2 = (bf16[8,256,512]{2,1,0:T(8,128)(2,1)}, bf16[8,256,512]{2,1,0:T(8,128)(2,1)}, u32[]{:S(2)}, u32[]{:S(2)}) collective-permute-start(bf16[8,256,512]{2,1,0:T(8,128)(2,1)} %collective-permute-done.1), channel_id=1, source_target_pairs={{0,1},{1,2},{2,3},{3,0},{4,5},{5,6},{6,7},{7,4},{8,9},{9,10},{10,1... | collective-permute-start | bytes 6291464 | tf_op jit(solution)/shard_map/ppermute | solution.py:202
  225.0 59.2 %all-to-all-start.2 = ((bf16[8,256,512]{2,1,0:T(8,128)(2,1)}), bf16[8,256,512]{2,1,0:T(8,128)(2,1)}, u32[]{:S(2)}, u32[]{:S(2)}) async-start(bf16[8,256,512]{2,1,0:T(8,128)(2,1)} %collective-permute-done), calls=%async_computation.2 | async-start | bytes 4194304 | tf_op jit(solution)/shard_map/all_to_all | solution.py:203
  229.4 54.1 %copy-start.1 = (bf16[8,256,512]{2,1,0:T(8,128)(2,1)S(1)}, bf16[8,256,512]{2,1,0:T(8,128)(2,1)}, u32[]{:S(2)}) copy-start(bf16[8,256,512]{2,1,0:T(8,128)(2,1)} %copy-done) | copy-start | bytes 6291460
  283.5 59.6 %collective-permute-start.3 = (bf16[8,256,512]{2,1,0:T(8,128)(2,1)S(1)}, bf16[8,256,512]{2,1,0:T(8,128)(2,1)}, u32[]{:S(2)}, u32[]{:S(2)}) collective-permute-start(bf16[8,256,512]{2,1,0:T(8,128)(2,1)S(1)} %copy-done.1), channel_id=1, source_target_pairs={{0,1},{1,2},{2,3},{3,0},{4,5},{5,6},{6,7},{7,4},{8,9},{9,10},{10,1... | collective-permute-start | bytes 6291464 | tf_op jit(solution)/shard_map/ppermute | solution.py:202
  284.2 61.0 %all-to-all-start.3 = ((bf16[8,256,512]{2,1,0:T(8,128)(2,1)}), bf16[8,256,512]{2,1,0:T(8,128)(2,1)}, u32[]{:S(2)}, u32[]{:S(2)}) async-start(bf16[8,256,512]{2,1,0:T(8,128)(2,1)} %collective-permute-done.1), calls=%async_computation.3 | async-start | bytes 4194304 | tf_op jit(solution)/shard_map/all_to_all | solution.py:203
  343.1 60.8 %collective-permute-start.4 = (bf16[8,256,512]{2,1,0:T(8,128)(2,1)}, bf16[8,256,512]{2,1,0:T(8,128)(2,1)}, u32[]{:S(2)}, u32[]{:S(2)}) collective-permute-start(bf16[8,256,512]{2,1,0:T(8,128)(2,1)} %collective-permute-done.3), channel_id=1, source_target_pairs={{0,1},{1,2},{2,3},{3,0},{4,5},{5,6},{6,7},{7,4},{8,9},{9,10},{10,1... | collective-permute-start | bytes 6291464 | tf_op jit(solution)/shard_map/ppermute | solution.py:202
  345.2 60.5 %all-to-all-start.4 = ((bf16[8,256,512]{2,1,0:T(8,128)(2,1)}), bf16[8,256,512]{2,1,0:T(8,128)(2,1)S(1)}, u32[]{:S(2)}, u32[]{:S(2)}) async-start(bf16[8,256,512]{2,1,0:T(8,128)(2,1)} %collective-permute-done.2), calls=%async_computation.4 | async-start | bytes 4194304 | tf_op jit(solution)/shard_map/all_to_all | solution.py:203
  404.0 166.5 %collective-permute-start.5 = (bf16[8,256,512]{2,1,0:T(8,128)(2,1)}, bf16[8,256,512]{2,1,0:T(8,128)(2,1)}, u32[]{:S(2)}, u32[]{:S(2)}) collective-permute-start(bf16[8,256,512]{2,1,0:T(8,128)(2,1)} %collective-permute-done.4), channel_id=1, source_target_pairs={{0,1},{1,2},{2,3},{3,0},{4,5},{5,6},{6,7},{7,4},{8,9},{9,10},{10,1... | collective-permute-start | bytes 6291464 | tf_op jit(solution)/shard_map/ppermute | solution.py:202
  405.7 1.3 copy-start.2
Sparse Core Ops, SparseCore 0:
  35.4 125.2 all-gather.2
